TPU v7x, 256 devices: a whole 4x4x8 slice. The times are simulated.
256 devices in a mesh: pole: 4 (over y), row: 8 (over z_lo, core), col: 8 (over x, z_hi).
Axes of the slice: x: 4, y: 4, z: 8 (z_hi: 2, z_lo: 4; z = z_hi * 4 + z_lo), core: 2. Of those that a mesh axis runs over, the one named last changes fastest.
Arguments:
- inverse_tiles: float32 [8, 2, 8, 512, 4096], P('pole', None, None, 'col', 'row'), may hold values from -6 to 6
- factor_block: float32 [8, 2, 4096, 512], P('pole', None, ('row', 'col')), may hold values from -0.09375 to 0.09375
- diag_inverse: float32 [8, 2, 2, 256, 256], P('pole'), may hold values from -6 to 6
- tile_pattern: int32 [64, 64], replicated, may hold values 0 or 1
- ancestor_blocks: int32 [2, 64], replicated, may hold values 0 or 1
- row_owner: int32 [4096, 1], P(('row', 'col')), may hold values from 0 to 3; in each aligned block of 64 rows (0 to 63, 64 to 127, ...) at most 32 rows name the same one
- pole_weights: float32 [8, 2], replicated, may hold values from -4 to 4
- pole_order: int32 [8], replicated, may hold values from 0 to 7, each once
Outputs:
- inverse_rows: float32 [8, 2, 4096, 512], P('pole', None, ('row', 'col'))
- owned_density: float32 [4, 2048, 512], P('pole', ('row', 'col'))
- block_density: float32 [2, 256, 256], replicated
Inputs may be any that keep to these rules, and one draw needn't show every extreme that they name: `row_owner`: in each aligned block of 64 rows (the rows of one device) no owner has more than 32 rows, and some owner has exactly 32 in some block.
All inputs are finite; a program needn't handle non-finite values.
Results may differ from a plain program's by a relative error of at most 0.000073.
Values sent between devices are 32-bit elements; how exact they have to be, the bound alone decides.
A program may use at most 64 MiB of HBM per device.

v0:
```python
import jax
import jax.numpy as jnp
from jax import lax
from jax.sharding import PartitionSpec as P


def product_high(left, right):
    return jnp.einsum("pts,psw->ptw", left, right, precision=lax.Precision.HIGHEST)


def contract(first, second):
    return jnp.einsum("pbks,pbkt->pkst", first, second, precision=lax.Precision.HIGHEST)


def shards(
    inverse_tiles,
    factor_block,
    diag_inverse,
    tile_pattern,
    ancestor_blocks,
    row_owner,
    pole_weights,
    pole_order,
):
    row_count = lax.axis_size("row")
    col_count = lax.axis_size("col")
    pole_total = lax.axis_size("pole")
    row_index = lax.axis_index("row")
    col_index = lax.axis_index("col")
    pole_index = lax.axis_index("pole")
    pole_count = inverse_tiles.shape[0]
    block_rows = inverse_tiles.shape[3]
    seg_cols = inverse_tiles.shape[4]
    width = factor_block.shape[3]
    supers = ancestor_blocks.shape[0]
    super_cols = width // supers
    own_block = row_index * col_count + col_index
    pattern_grid = tile_pattern.reshape(row_count, col_count, row_count, col_count).astype(
        jnp.float32
    )
    rows_pick = lax.dynamic_index_in_dim(pattern_grid, col_index, 1, keepdims=False)
    tiles_here = lax.dynamic_index_in_dim(rows_pick, row_index, 1, keepdims=False)
    col_keep = jnp.repeat(tiles_here, block_rows, axis=1)
    masked = inverse_tiles * col_keep[None, None, :, None, :]
    flattened = masked.reshape(pole_count, 2, row_count * block_rows, seg_cols)
    anc_keep = lax.dynamic_index_in_dim(ancestor_blocks, own_block, 1, keepdims=False).astype(
        jnp.float32
    )
    width_keep = jnp.repeat(anc_keep, super_cols)
    factor = factor_block * width_keep
    fac_piece = lax.all_gather(factor, "col", axis=2, tiled=True)
    real_part = product_high(flattened[:, 0], fac_piece[:, 0]) - product_high(
        flattened[:, 1], fac_piece[:, 1]
    )
    imag_part = product_high(flattened[:, 0], fac_piece[:, 1]) + product_high(
        flattened[:, 1], fac_piece[:, 0]
    )
    partial_value = jnp.stack([real_part, imag_part], axis=1)
    inverse_rows = (
        lax.psum_scatter(partial_value, "row", scatter_dimension=2, tiled=True) * width_keep
    )
    fac_split = factor.reshape(pole_count, 2, block_rows, supers, super_cols)
    rows_split = inverse_rows.reshape(pole_count, 2, block_rows, supers, super_cols)
    prod_real = contract(fac_split[:, 0], rows_split[:, 0]) - contract(
        fac_split[:, 1], rows_split[:, 1]
    )
    prod_imag = contract(fac_split[:, 0], rows_split[:, 1]) + contract(
        fac_split[:, 1], rows_split[:, 0]
    )
    order_here = lax.dynamic_slice_in_dim(pole_order, pole_index * pole_count, pole_count)
    table_hot = (
        order_here[:, None] == jnp.arange(pole_order.shape[0], dtype=jnp.int32)[None, :]
    ).astype(jnp.float32)
    weights = jnp.dot(
        table_hot, pole_weights, precision=lax.Precision.HIGHEST, preferred_element_type=jnp.float32
    )
    weight_real = weights[:, 0]
    weight_imag = weights[:, 1]
    summed_real, summed_imag = lax.psum((prod_real, prod_imag), ("row", "col"))
    green_real = diag_inverse[:, 0] - summed_real
    green_imag = diag_inverse[:, 1] - summed_imag
    local_kk = jnp.sum(
        weight_real[:, None, None, None] * green_imag
        + weight_imag[:, None, None, None] * green_real,
        axis=0,
    )
    block_density = lax.psum(local_kk, "pole")
    dens_local = jnp.sum(
        weight_real[:, None, None] * inverse_rows[:, 1]
        + weight_imag[:, None, None] * inverse_rows[:, 0],
        axis=0,
    )
    owner_ids = row_owner[:, 0]
    owner_hot = (owner_ids[:, None] == jnp.arange(pole_total, dtype=jnp.int32)[None, :]).astype(
        jnp.int32
    )
    owner_rank = jnp.cumsum(owner_hot, axis=0) - owner_hot
    rank_own = jnp.sum(owner_hot * owner_rank, axis=1)
    capacity = block_rows // 2
    slot_hit = (rank_own[:, None] == jnp.arange(capacity, dtype=jnp.int32)[None, :]).astype(
        jnp.float32
    )
    selector = jnp.transpose(
        owner_hot.astype(jnp.float32)[:, :, None] * slot_hit[:, None, :], (1, 2, 0)
    )
    summed_rows = lax.psum(dens_local, "pole")
    my_select = lax.dynamic_index_in_dim(selector, pole_index, 0, keepdims=True)
    owned_density = jnp.einsum(
        "pst,tw->psw", my_select, summed_rows, precision=lax.Precision.HIGHEST
    )
    return (inverse_rows, owned_density, block_density)


def solution(mesh):
    placed = (
        P("pole", None, None, "col", "row"),
        P("pole", None, ("row", "col"), None),
        P("pole", None, None, None, None),
        P(),
        P(),
        P(("row", "col"), None),
        P(),
        P(),
    )
    return jax.shard_map(
        shards,
        mesh=mesh,
        in_specs=placed,
        out_specs=(P("pole", None, ("row", "col"), None), P("pole", ("row", "col"), None), P()),
        check_vma=False,
    )
```

profile of v0, /device:TPU:1, one launch (start us, length us, event | category | flops | bytes accessed | tf_op | source)
XLA Modules:
  0.0 448.7 jit_solution(11839752003630871838)
XLA Ops:
  7.2 0.9 convert_reduce_fusion
  8.2 1.9 copy_multiply_fusion
  10.1 0.8 convert_element_type.34
  11.2 2.9 broadcast_multiply_fusion
  14.2 2.5 copy.20
  16.7 104.9 %all-gather.2.cloned.1.call-done = f32[2,2,512,512]{3,2,0,1:T(8,128)} async-done(((f32[2,2,64,512]{3,2,0,1:T(8,128)}), f32[2,2,512,512]{3,2,0,1:T(8,128)}) %all-gather.2.cloned.1.call-update) | async-done | bytes 4194320 | tf_op jit(solution)/shard_map/all_gather | solution.py:51
  121.6 5.9 %fusion.1 = f32[2,512,512]{2,1,0:T(8,128)S(1)} fusion(f32[2,2,512,512]{3,2,0,1:T(8,128)} %bitcast.98, f32[2,2,512,512]{3,2,0,1:T(8,128)} %all-gather.2.cloned.1.call-done), kind=kOutput, calls=%fused_computation.9 | convolution fusion | flops 3221225472 | bytes 6291456 | tf_op jit(solution)/shard_map/pts,psw->ptw/dot_general | solution.py:8
  127.5 5.3 %fusion = f32[2,512,512]{2,1,0:T(8,128)S(1)} fusion(f32[2,2,512,512]{3,2,0,1:T(8,128)S(1)} %bitcast.99, f32[2,2,512,512]{3,2,0,1:T(8,128)} %all-gather.2.cloned.1.call-done), kind=kOutput, calls=%fused_computation.8 | convolution fusion | flops 3221225472 | bytes 6291456 | tf_op jit(solution)/shard_map/pts,psw->ptw/dot_general | solution.py:8
  132.8 3.6 subtract_bitcast_fusion
  136.4 3.7 add_bitcast_fusion
  140.1 2.4 pad_maximum_fusion
  142.6 1.0 copy-done.3
  144.1 46.5 %reduce-scatter.2.cloned.1.call-done = f32[2,2,64,512]{3,2,0,1:T(8,128)} async-done(((f32[2,2,512,512]{3,2,0,1:T(8,128)}), f32[2,2,64,512]{3,2,0,1:T(8,128)}) %reduce-scatter.2.cloned.1.call-update) | async-done | bytes 524304 | tf_op jit(solution)/shard_map/reduce_scatter | solution.py:60
  190.6 1.1 broadcast_multiply_fusion.1
  192.3 1.1 fusion.13
  193.3 1.1 fusion.12
  194.4 2.1 convolution_add_fusion
  196.5 2.1 convolution_subtract_fusion
  200.0 187.8 %all-reduce.5.cloned.1.call-done = (f32[2,2,256,256]{3,2,1,0:T(8,128)}, f32[2,2,256,256]{3,2,1,0:T(8,128)}) async-done(((f32[2,2,256,256]{3,2,1,0:T(8,128)}, f32[2,2,256,256]{3,2,1,0:T(8,128)}), (f32[2,2,256,256]{3,2,1,0:T(8,128)}, f32[2,2,256,256]{3,2,1,0:T(8,128)})) %all-reduce.5.cloned.1.call-update) | async-done | bytes 2097168 | tf_op jit(solution)/shard_map/psum | solution.py:79
  387.9 3.0 fusion.6
  391.4 0.8 copy.28
  392.2 46.2 %all-reduce.7.cloned.1.call-done = (f32[64,512]{1,0:T(8,128)}, f32[2,256,256]{2,1,0:T(8,128)}) async-done(((f32[64,512]{1,0:T(8,128)}, f32[2,256,256]{2,1,0:T(8,128)}), (f32[64,512]{1,0:T(8,128)}, f32[2,256,256]{2,1,0:T(8,128)})) %all-reduce.7.cloned.1.call-update) | async-done | bytes 655376 | tf_op jit(solution)/shard_map/psum | solution.py:106
  438.5 1.8 convolution_bitcast_fusion
  440.3 1.9 copy.53
  (41 shorter events, 3.5 us)
Async XLA Ops:
  7.2 191.7 %copy-start = (f32[8,2]{0,1:T(2,128)S(1)}, f32[8,2]{0,1:T(2,128)}, u32[]{:S(2)}) copy-start(f32[8,2]{0,1:T(2,128)} %param.14) | copy-start | bytes 196
  7.2 114.4 %all-gather.2.cloned.1.call-start = ((), (), s32[]{:S(2)}) async-start(), calls=%async_computation.1 | async-start | bytes 4718592 | tf_op jit(solution)/shard_map/all_gather | solution.py:51
  10.1 180.6 %reduce-scatter.2.cloned.1.call-start = ((), (), s32[]{:S(2)}) async-start(), calls=%async_computation.2 | async-start | bytes 4718592 | tf_op jit(solution)/shard_map/reduce_scatter | solution.py:60
  121.6 5.9 %copy-start.1 = (f32[2,2,8,64,512]{4,3,2,0,1:T(8,128)S(1)}, f32[2,2,8,64,512]{4,3,2,0,1:T(8,128)}, u32[]{:S(2)}) copy-start(f32[2,2,8,64,512]{4,3,2,0,1:T(8,128)} %copy.20) | copy-start | bytes 12582916
  127.5 5.3 %copy-start.2 = (f32[2,2,512,512]{3,2,0,1:T(8,128)S(1)}, f32[2,2,512,512]{3,2,0,1:T(8,128)}, u32[]{:S(2)}) copy-start(f32[2,2,512,512]{3,2,0,1:T(8,128)} %all-gather.2.cloned.1.call-done) | copy-start | bytes 12582916
  142.5 1.0 copy-start.3
  142.5 245.3 %all-reduce.5.cloned.1.call-start = ((), (), s32[]{:S(2)}) async-start(), calls=%async_computation.3 | async-start | bytes 4194304 | tf_op jit(solution)/shard_map/psum | solution.py:79
  196.5 2.2 copy-start.5
  196.5 2.3 copy-start.6
  198.5 189.3 %copy-start.4 = (f32[2,2,2,256,256]{4,3,2,1,0:T(8,128)S(1)}, f32[2,2,2,256,256]{4,3,2,1,0:T(8,128)}, u32[]{:S(2)}) copy-start(f32[2,2,2,256,256]{4,3,2,1,0:T(8,128)} %param.10) | copy-start | bytes 6291460
  198.6 239.9 %all-reduce.7.cloned.1.call-start = ((), (), s32[]{:S(2)}) async-start(), calls=%async_computation.4 | async-start | bytes 1310720 | tf_op jit(solution)/shard_map/psum | solution.py:106
Sparse Core Ops, SparseCore 0:
  11.2 110.3 all-gather.1
  142.7 47.9 reduce-scatter.1
  198.7 189.1 all-reduce.4
  391.0 47.4 all-reduce.6
where the time goes:
time: 450 us; the launch traced here: 449 us
  waiting for transfers between devices  386 us (86%)
  matrix products  26.7 us (6%)
  other arithmetic  14.2 us (3%)
  between operations  14 us (3%)
  local copies, waits for them, and re-layouts  7.98 us (2%)
    psum x1, waiting for transfers between devices, shards(): summed_real, summed_imag = lax.psum((prod_real, prod_imag), ('row', 'col'))  188 us
    all_gather x1, waiting for transfers between devices, shards(): fac_piece = lax.all_gather(factor, 'col', axis=2, tiled=True)  105 us
    reduce_scatter x1, waiting for transfers between devices, shards(): lax.psum_scatter(partial_value, 'row', scatter_dimension=2, tiled=True)  46.5 us
    psum x1, waiting for transfers between devices, shards(): summed_rows = lax.psum(dens_local, 'pole')  46.2 us
    dot_general x4, matrix products, product_high(): jnp.einsum('pts,psw->ptw', left, right, precision=lax.Precision.HIGHEST)  18.5 us
  transfers between devices with their start and end apart: 4, of which 4 were waited for; matrix products, arithmetic and copies ran while one was open for 2% of the time, Pallas kernels for 0%

commit v1 on v0

v1 whole, which is shorter than its diff:
```python
import functools

import jax
import jax.numpy as jnp
from jax import lax
from jax.experimental import pallas as pl
from jax.experimental.pallas import tpu as pltpu
from jax.sharding import PartitionSpec as P

MESH = pl.DeviceIdType.MESH
JOBS = ((0, 0), (1, 0), (0, 1), (1, 1))
NJ = len(JOBS)
F32, BF16 = jnp.float32, jnp.bfloat16


def split(value):
    high = value.astype(BF16)
    return high, (value - high.astype(F32)).astype(BF16)


def dot(left, right):
    return jnp.dot(left, right, preferred_element_type=F32)


def main_kernel(
    tiles_hbm, diag_hbm, factor, pattern, owner, anc, order, table,
    rows_out, dens_out, zed_out,
    tiles, diag, dens, zed, zcross, zpart, zplane, zline, chosen, picked, dgot, a_high, a_low, gath, l_high, l_low, prod, cross, sums, line, tile_sem, diag_sem,
    zs, zr, xs, xr, fs, fr, cs, cr, ls, lr,
    t0s, t0r, t1s, t1r, t2s, t2r, t3s, t3r, t4s, t4r, ds, dr,
):
    pole, row, col = lax.axis_index("pole"), lax.axis_index("row"), lax.axis_index("col")
    zl, core = row // 2, row % 2
    x, zh = col // 2, col % 2
    half = zl // 2
    inner = zl + half * (3 - 2 * zl)
    other_col = x * 2 + 1 - zh
    right_x, left_x = (x + 1) % 4, (x + 3) % 4

    partner = (pole, row, other_col)
    right = (pole, row, right_x * 2 + zh)
    left = (pole, row, left_x * 2 + zh)
    sibling = (pole, zl * 2 + 1 - core, col)
    mate = (pole, (1 - inner + half * (1 + 2 * inner)) * 2 + core, col)
    across = (pole, (3 - zl) * 2 + core, col)

    load = pltpu.make_async_copy(tiles_hbm, tiles, tile_sem)
    load.start()

    plane_at = pole * 4 + x
    z_at = zh * 4 + zl
    diag_load = pltpu.make_async_copy(
        diag_hbm.at[:, :, :, core * 16 + x * 4 + zl], diag, diag_sem
    )
    diag_load.start()

    def plane_peer(i):
        at = (plane_at + i) % 16
        return at, (at // 4, row, (at % 4) * 2 + zh)

    def line_peer(i):
        at = (z_at + i) % 8
        return (pole, (at % 4) * 2 + core, x * 2 + at // 4)

    barrier = pltpu.get_barrier_semaphore()

    def greet_plane(i, carry):
        pl.semaphore_signal(barrier, inc=1, device_id=plane_peer(i)[1], device_id_type=MESH)
        return carry

    def greet_line(i, carry):
        pl.semaphore_signal(barrier, inc=1, device_id=line_peer(i), device_id_type=MESH)
        return carry

    lax.fori_loop(1, 16, greet_plane, 0)
    lax.fori_loop(1, 8, greet_line, 0)
    pl.semaphore_signal(barrier, inc=1, device_id=sibling, device_id_type=MESH)

    block = row * 8 + col
    keeps = [anc[k, block].astype(F32) for k in range(2)]
    for j, (p, k) in enumerate(JOBS):
        gath[j, col] = factor[p, :, :, k * 256 : (k + 1) * 256] * keeps[k]

    pl.semaphore_wait(barrier, 23)

    def remote(src, dst, send, recv, peer):
        return pltpu.make_async_remote_copy(
            src_ref=src, dst_ref=dst, send_sem=send, recv_sem=recv, device_id=peer, device_id_type=MESH
        )

    def z_copy(j):
        return remote(gath.at[j, col], gath.at[j, col], zs.at[j], zr.at[j], partner)

    def z_recv(j):
        return remote(gath.at[j, other_col], gath.at[j, other_col], zs.at[j], zr.at[j], partner)

    def x_copy(j, h, d):
        slot = col if h == 0 else other_col
        peer = right if d == 0 else left
        return remote(gath.at[j, slot], gath.at[j, slot], xs.at[j, h, d], xr.at[j, h, d], peer)

    def x_slot(h, shift):
        half_of = zh if h == 0 else 1 - zh
        return ((x + shift) % 4) * 2 + half_of

    def x_recv(j, h, d):
        slot = x_slot(h, 3 if d == 0 else 1)
        return remote(gath.at[j, slot], gath.at[j, slot], xs.at[j, h, d], xr.at[j, h, d], right)

    def f_copy(j, h, d):
        slot = x_slot(h, 3 if d == 0 else 1)
        peer = right if d == 0 else left
        return remote(gath.at[j, slot, d], gath.at[j, slot, d], fs.at[j, h, d], fr.at[j, h, d], peer)

    def f_recv(j, h, d):
        slot = x_slot(h, 2)
        return remote(gath.at[j, slot, d], gath.at[j, slot, d], fs.at[j, h, d], fr.at[j, h, d], right)

    def z_forward(j):
        z_recv(j).wait_recv()
        for d in range(2):
            x_copy(j, 1, d).start()

    def x_forward(j, h):
        for d in range(2):
            x_recv(j, h, d).wait_recv()
            f_copy(j, h, d).start()

    def f_wait(j):
        for h in range(2):
            for d in range(2):
                f_recv(j, h, d).wait_recv()

    def prepare():
        load.wait()
        expand = (
            lax.broadcasted_iota(jnp.int32, (64, 512), 0)
            == row * 8 + lax.broadcasted_iota(jnp.int32, (64, 512), 1) // 64
        ).astype(BF16)
        tile_rows = jnp.concatenate(
            [pattern[pl.ds(g * 8 + col, 1), :] for g in range(8)], axis=0
        ).astype(F32).astype(BF16)
        keep_cols = dot(tile_rows, expand)
        for g in range(8):
            mask = keep_cols[g : g + 1, :]

            def one(i, carry, g=g, mask=mask):
                p, part = i // 2, i % 2
                high, low = split(tiles[p, part, g] * mask)
                a_high[p, part, g * 64 : (g + 1) * 64] = high
                a_low[p, part, g * 64 : (g + 1) * 64] = low
                return carry

            lax.fori_loop(0, 4, one, 0)

    def multiply(j):
        p, k = JOBS[j]

        def halves(c, carry):
            for part in range(2):
                high, low = split(gath[j, c, part])
                at = pl.ds(pl.multiple_of(c * 64, 64), 64)
                l_high[part, at] = high
                l_low[part, at] = low
                if part == 1:
                    l_high[2, at] = -high
                    l_low[2, at] = -low
            return carry

        lax.fori_loop(0, 8, halves, 0)

        def one(n, carry):
            total = None
            for part in range(2):
                pick = part * 2 * (1 - n) + (1 - part) * n
                bh, bl = l_high[pick], l_low[pick]
                ah, al = a_high[p, part], a_low[p, part]
                term = dot(ah, bh) + (dot(ah, bl) + dot(al, bh))
                total = term if total is None else total + term
            for g in range(8):
                prod[j, g, n] = total[g * 64 : (g + 1) * 64]
            return carry

        lax.fori_loop(0, 2, one, 0)
        for d in range(4):
            c_copy(j, d).start()

    def c_copy(j, d):
        return remote(prod.at[j, d * 2 + 1 - core], cross.at[j, d], cs.at[j, d], cr.at[j, d], sibling)

    def at_line(d):
        return d + half * (3 - 2 * d)

    def l_copy(j, slot, d, peer):
        return remote(sums.at[j, d], line.at[j, slot], ls.at[j, d], lr.at[j, slot], peer)

    def l_wait(j, slot):
        remote(sums.at[j, 0], line.at[j, slot], ls.at[j, 0], lr.at[j, slot], mate).wait_recv()

    def c_sum(j):
        for d in (3, 2, 1, 0):
            place = at_line(d)
            remote(prod.at[j, 0], cross.at[j, place], cs.at[j, d], cr.at[j, place], sibling).wait_recv()
            sums[j, d] = prod[j, place * 2 + core] + cross[j, place]
            if d > 0:

                @pl.when(inner == 0)
                def _(d=d):
                    l_copy(j, d - 1, d, mate).start()

    def l_mid(j):
        @pl.when(inner == 1)
        def _():
            for d in (3, 2):
                l_wait(j, d - 1)
                sums[j, d] = sums[j, d] + line[j, d - 1]
                l_copy(j, 6 - d, d, across).start()

    def l_end(j):
        @pl.when(inner == 1)
        def _():
            l_wait(j, 3)
            sums[j, 0] = sums[j, 0] + line[j, 3]
            l_copy(j, 3, 0, mate).start()
            l_wait(j, 0)
            l_wait(j, 4)
            sums[j, 1] = sums[j, 1] + (line[j, 0] + line[j, 4])

        @pl.when(inner == 0)
        def _():
            l_wait(j, 3)
            sums[j, 0] = sums[j, 0] + line[j, 3]

    def output(j):
        p, k = JOBS[j]
        at = slice(k * 256, (k + 1) * 256)
        done = sums[j, inner] * keeps[k]
        rows_out[p, :, :, at] = done
        entry = order[pole * 2 + p]
        wr, wi = table[entry, 0], table[entry, 1]
        fr_, fi_ = gath[j, col, 0], gath[j, col, 1]
        density = wr * done[1] + wi * done[0]
        left_side = jnp.concatenate([wr * fi_ + wi * fr_, wr * fr_ - wi * fi_], axis=0)
        right_side = jnp.concatenate([done[0], done[1]], axis=0)
        product = lax.dot_general(
            left_side, right_side, (((0,), (0,)), ((), ())),
            precision=lax.Precision.HIGHEST, preferred_element_type=F32,
        ).reshape(32, 8, 256)
        if p == 0:
            dens[k] = density
            zed[k] = -product
        else:
            dens[k] += density
            zed[k] -= product

    def choose():
        lanes = lax.broadcasted_iota(jnp.int32, (64, 128), 1)
        hot = (owner[...] == lanes // 32).astype(F32)
        before = (
            lax.broadcasted_iota(jnp.int32, (64, 64), 1) < lax.broadcasted_iota(jnp.int32, (64, 64), 0)
        ).astype(BF16)
        rank = dot(before, hot.astype(BF16))
        chosen[...] = jnp.where(rank == (lanes % 32).astype(F32), hot, 0.0)

    def d_copy(k, i):
        to = (pole + i) % 4
        return remote(picked.at[k, to], dgot.at[k, i - 1], ds.at[k], dr.at[k], (to, row, col))

    def d_send(k):
        picked[k] = lax.dot_general(
            chosen[...], dens[k], (((0,), (0,)), ((), ())),
            precision=lax.Precision.HIGHEST, preferred_element_type=F32,
        ).reshape(4, 32, 256)
        for i in range(1, 4):
            d_copy(k, i).start()

    def d_all(k):
        return remote(picked.at[k, 0:3], dgot.at[k], ds.at[k], dr.at[k], sibling)

    def d_take(k):
        d_all(k).wait_recv()
        dens_out[:, k * 256 : (k + 1) * 256] = picked[k, pole] + (dgot[k, 0] + dgot[k, 1] + dgot[k, 2])

    def t0_copy(k):
        return remote(zed.at[k, pl.ds((1 - core) * 16, 16)], zcross.at[k], t0s.at[k], t0r.at[k], sibling)

    def t1_send(k):
        t0_copy(k).wait_recv()
        zpart[k] = zed[k, pl.ds(core * 16, 16)] + zcross[k]

        @pl.when(zh == 0)
        def _():
            here = x * 4 + zl
            part = zpart[k, here]
            for p in range(2):
                entry = order[pole * 2 + p]
                part = part + (table[entry, 0] * diag[p, 1, k] + table[entry, 1] * diag[p, 0, k])
            zpart[k, here] = part

        def send(i, carry):
            at, peer = plane_peer(i)
            remote(zpart.at[k, at], zplane.at[k, i - 1], t1s.at[k], t1r.at[k], peer).start()
            return carry

        lax.fori_loop(1, 16, send, 0)

    def t1_all(k):
        return remote(zpart.at[k, 0:15], zplane.at[k], t1s.at[k], t1r.at[k], sibling)

    def t2_send(k):
        t1_all(k).wait_recv()
        zline[k, z_at] = zpart[k, plane_at] + jnp.sum(zplane[k], axis=0)

        def send(i, carry):
            here = zline.at[k, z_at]
            remote(here, here, t2s.at[k], t2r.at[k], line_peer(i)).start()
            return carry

        lax.fori_loop(1, 8, send, 0)

    def t2_all(k):
        return remote(zline.at[k, 0:7], zline.at[k, 0:7], t2s.at[k], t2r.at[k], sibling)

    def t3_send(k):
        t2_all(k).wait_recv()
        mine = zed_out.at[k, core * 16 + plane_at]
        mine[...] = jnp.sum(zline[k], axis=0)

        def send(i, carry):
            remote(mine, mine, t3s.at[k], t3r.at[k], plane_peer(i)[1]).start()
            return carry

        lax.fori_loop(1, 16, send, 0)

    def t3_all(k):
        here = zed_out.at[k, pl.ds(core * 16, 15)]
        return remote(here, here, t3s.at[k], t3r.at[k], sibling)

    def t4_copy(k):
        here = zed_out.at[k, pl.ds(core * 16, 16)]
        return remote(here, here, t4s.at[k], t4r.at[k], sibling)

    def t4_send(k):
        t3_all(k).wait_recv()
        t4_copy(k).start()

    def sum_start(k):
        t0_copy(k).start()
        d_send(k)

    for j in range(NJ):
        z_copy(j).start()
        for d in range(2):
            x_copy(j, 0, d).start()
    prepare()
    choose()
    diag_load.wait()
    x_forward(0, 0)
    z_forward(0)
    x_forward(1, 0)
    for j in range(NJ):
        x_forward(j, 1)
        if j + 1 < NJ:
            z_forward(j + 1)
        if j + 2 < NJ:
            x_forward(j + 2, 0)
        f_wait(j)
        multiply(j)
        if j >= 1:
            l_mid(j - 1)
        c_sum(j)
        if j >= 1:
            l_end(j - 1)
            output(j - 1)
        if j == 2:
            sum_start(0)
        if j == 3:
            t1_send(0)
    l_mid(NJ - 1)
    t2_send(0)
    l_end(NJ - 1)
    output(NJ - 1)
    sum_start(1)
    t3_send(0)
    t1_send(1)
    t4_send(0)
    t2_send(1)
    d_take(0)
    d_take(1)
    t3_send(1)
    t4_send(1)
    for k in range(2):
        t4_copy(k).wait_recv()

    for k in range(2):
        for copy in (t0_copy(k), t1_all(k), t2_all(k), t3_all(k), t4_copy(k), d_all(k)):
            copy.wait_send()
    for j in range(NJ):
        z_copy(j).wait_send()
        for h in range(2):
            for d in range(2):
                x_copy(j, h, d).wait_send()
                f_copy(j, h, d).wait_send()
        for d in range(4):
            c_copy(j, d).wait_send()

        @pl.when(inner == 0)
        def _(j=j):
            for d in (3, 2, 1):
                l_copy(j, d - 1, d, mate).wait_send()

        @pl.when(inner == 1)
        def _(j=j):
            for d in (3, 2, 0):
                l_copy(j, 0, d, mate).wait_send()


def main_call(tiles, diag, factor, pattern, owner, anc, order, table):
    vmem = pl.BlockSpec(memory_space=pltpu.VMEM)
    smem = pl.BlockSpec(memory_space=pltpu.SMEM)
    hbm = pl.BlockSpec(memory_space=pl.ANY)
    dma = pltpu.SemaphoreType.DMA
    return pl.pallas_call(
        main_kernel,
        out_shape=(
            jax.ShapeDtypeStruct((2, 2, 64, 512), F32),
            jax.ShapeDtypeStruct((32, 512), F32),
            jax.ShapeDtypeStruct((2, 32, 8, 256), F32),
        ),
        in_specs=[hbm, hbm, vmem, vmem, vmem, smem, smem, smem],
        out_specs=(vmem, vmem, vmem),
        scratch_shapes=[
            pltpu.VMEM((2, 2, 8, 64, 512), F32),
            pltpu.VMEM((2, 2, 2, 8, 256), F32),
            pltpu.VMEM((2, 64, 256), F32),
            pltpu.VMEM((2, 32, 8, 256), F32),
            pltpu.VMEM((2, 16, 8, 256), F32),
            pltpu.VMEM((2, 16, 8, 256), F32),
            pltpu.VMEM((2, 15, 8, 256), F32),
            pltpu.VMEM((2, 8, 8, 256), F32),
            pltpu.VMEM((64, 128), F32),
            pltpu.VMEM((2, 4, 32, 256), F32),
            pltpu.VMEM((2, 3, 32, 256), F32),
            pltpu.VMEM((2, 2, 512, 512), BF16),
            pltpu.VMEM((2, 2, 512, 512), BF16),
            pltpu.VMEM((NJ, 8, 2, 64, 256), F32),
            pltpu.VMEM((3, 512, 256), BF16),
            pltpu.VMEM((3, 512, 256), BF16),
            pltpu.VMEM((NJ, 8, 2, 64, 256), F32),
            pltpu.VMEM((NJ, 4, 2, 64, 256), F32),
            pltpu.VMEM((NJ, 4, 2, 64, 256), F32),
            pltpu.VMEM((NJ, 5, 2, 64, 256), F32),
            dma, dma,
            dma((NJ,)), dma((NJ,)),
            dma((NJ, 2, 2)), dma((NJ, 2, 2)),
            dma((NJ, 2, 2)), dma((NJ, 2, 2)),
            dma((NJ, 4)), dma((NJ, 4)),
            dma((NJ, 4)), dma((NJ, 5)),
            *([dma((2,))] * 12),
        ],
        compiler_params=pltpu.CompilerParams(
            collective_id=0, has_side_effects=True, vmem_limit_bytes=60 * 2**20
        ),
    )(tiles, diag, factor, pattern, owner, anc, order, table)


def shards(tiles, factor, diag, pattern, anc, row_owner, table, order):
    rows, dens, zed = main_call(
        tiles, diag.reshape(2, 2, 2, 32, 8, 256), factor, pattern, row_owner, anc, order, table
    )
    return rows, dens[None], zed.reshape(2, 256, 256)


def solution(mesh):
    placed = (
        P("pole", None, None, "col", "row"),
        P("pole", None, ("row", "col"), None),
        P("pole", None, None, None, None),
        P(),
        P(),
        P(("row", "col"), None),
        P(),
        P(),
    )
    return jax.shard_map(
        shards,
        mesh=mesh,
        in_specs=placed,
        out_specs=(P("pole", None, ("row", "col"), None), P("pole", ("row", "col"), None), P()),
        check_vma=False,
    )
```

time: 450 us -> 124 us (0.28)
  waiting for transfers between devices: 386 us -> 0 us
  Pallas kernels: 0 us -> 115 us
  matrix products: 26.7 us -> 0 us
  other arithmetic: 14.2 us -> 0 us
  between operations: 14 us -> 0.64 us
    psum x2 -> x0, waiting for transfers between devices: 234 us -> none  [the longest x1 188 us: shards(): summed_real, summed_imag = lax.psum((prod_real, prod_imag), ('row', 'col'))]
    pallas_call x0 -> x1, Pallas kernels: none -> 115 us  [main_call(): pl.pallas_call(main_kernel, out_shape=(jax.ShapeDtypeStruct((2, 2, 64, 51...]
    all_gather x1 -> x0, waiting for transfers between devices: 105 us -> none  [shards(): fac_piece = lax.all_gather(factor, 'col', axis=2, tiled=True)]
    reduce_scatter x1 -> x0, waiting for transfers between devices: 46.5 us -> none  [shards(): lax.psum_scatter(partial_value, 'row', scatter_dimension=2, tiled=True)]
    dot_general x10 -> x0, matrix products: 26.7 us -> none  [the longest x4 18.5 us: product_high(): jnp.einsum('pts,psw->ptw', left, right, precision=lax.Precision.HIGHEST)]
    mul x4 -> x0, other arithmetic: 6.04 us -> none  [the longest x1 2.93 us: shards(): masked = inverse_tiles * col_keep[None, None, :, None, :]]
  transfers between devices with their start and end apart: 4 -> 0, of which waited for: 4 -> 0; matrix products, arithmetic and copies ran while one was open for 2% -> 0% of each run, Pallas kernels for 0% -> 0%
where the time goes in v1:
time: 124 us
  Pallas kernels  115 us (93%)
  local copies, waits for them, and re-layouts  7.91 us (6%)
    pallas_call x1, Pallas kernels, main_call(): pl.pallas_call(main_kernel, out_shape=(jax.ShapeDtypeStruct((2, 2, 64, 51...  115 us
    unnamed x5, local copies, waits for them, and re-layouts  7.91 us

profile of v1, /device:TPU:1, one launch (start us, length us, event | category | flops | bytes accessed | tf_op | source)
XLA Modules:
  0.0 124.0 jit_solution(124378517793555853)
XLA Ops:
  0.6 1.3 %copy.12.table = f32[8,2]{1,0:T(8,128)} copy(f32[8,2]{0,1:T(2,128)} %param.14) | data formatting | bytes 128 | tf_op args[6]
  2.0 1.4 %copy.11.owner = s32[64,1]{1,0:T(8,128)} copy(s32[64,1]{0,1:T(1,128)} %param.13) | data formatting | bytes 512 | tf_op args[5]
  3.3 115.4 %shard_map.103 = (f32[2,2,64,512]{3,2,1,0:T(8,128)}, f32[32,512]{1,0:T(8,128)}, f32[2,32,8,256]{3,2,1,0:T(8,128)}) custom-call(f32[2,2,8,64,512]{4,3,2,1,0:T(8,128)} %tiles_hbm.1, f32[2,2,2,32,8,256]{5,4,3,2,1,0:T(8,128)} %bitcast.3, f32[2,2,64,512]{3,2,1,0:T(8,128)} %factor.1, s32[64,64]{1,0:T(8,128)} %pattern.1, s32[64,1]{1,0:T(8,128)} %copy.11.owner, ...), custom_call_target="tpu_custom_call" | custom-call | tf_op jit(solution)/shard_map/pallas_call | solution.py:423
  118.7 1.9 %copy.16 = f32[2,2,64,512]{3,2,1,0:T(8,128)} copy(f32[2,2,64,512]{3,2,1,0:T(8,128)} %get-tuple-element.12) | data formatting | bytes 1048576
  120.6 1.5 %copy.17 = f32[1,32,512]{2,1,0:T(8,128)} copy(f32[1,32,512]{2,1,0:T(8,128)} %bitcast.5) | data formatting | bytes 131072
  122.1 1.9 %copy.18 = f32[2,256,256]{2,1,0:T(8,128)} copy(f32[2,256,256]{2,1,0:T(8,128)} %bitcast.4) | data formatting | bytes 1048576

commit v2 on v1

--- a/solution.py
+++ b/solution.py
@@ -237,7 +237,7 @@
         done = sums[j, inner] * keeps[k]
         rows_out[p, :, :, at] = done
         entry = order[pole * 2 + p]
-        wr, wi = table[entry, 0], table[entry, 1]
+        wr, wi = table[0, entry], table[1, entry]
         fr_, fi_ = gath[j, col, 0], gath[j, col, 1]
         density = wr * done[1] + wi * done[0]
         left_side = jnp.concatenate([wr * fi_ + wi * fr_, wr * fr_ - wi * fi_], axis=0)
@@ -254,13 +254,13 @@
             zed[k] -= product
 
     def choose():
-        lanes = lax.broadcasted_iota(jnp.int32, (64, 128), 1)
-        hot = (owner[...] == lanes // 32).astype(F32)
+        lines = lax.broadcasted_iota(jnp.int32, (128, 64), 0)
+        hot = (owner[...] == lines // 32).astype(F32)
         before = (
-            lax.broadcasted_iota(jnp.int32, (64, 64), 1) < lax.broadcasted_iota(jnp.int32, (64, 64), 0)
+            lax.broadcasted_iota(jnp.int32, (64, 64), 0) < lax.broadcasted_iota(jnp.int32, (64, 64), 1)
         ).astype(BF16)
-        rank = dot(before, hot.astype(BF16))
-        chosen[...] = jnp.where(rank == (lanes % 32).astype(F32), hot, 0.0)
+        rank = dot(hot.astype(BF16), before)
+        chosen[...] = jnp.where(rank == (lines % 32).astype(F32), hot, 0.0)
 
     def d_copy(k, i):
         to = (pole + i) % 4
@@ -268,7 +268,7 @@
 
     def d_send(k):
         picked[k] = lax.dot_general(
-            chosen[...], dens[k], (((0,), (0,)), ((), ())),
+            chosen[...], dens[k], (((1,), (0,)), ((), ())),
             precision=lax.Precision.HIGHEST, preferred_element_type=F32,
         ).reshape(4, 32, 256)
         for i in range(1, 4):
@@ -294,7 +294,7 @@
             part = zpart[k, here]
             for p in range(2):
                 entry = order[pole * 2 + p]
-                part = part + (table[entry, 0] * diag[p, 1, k] + table[entry, 1] * diag[p, 0, k])
+                part = part + (table[0, entry] * diag[p, 1, k] + table[1, entry] * diag[p, 0, k])
             zpart[k, here] = part
 
         def send(i, carry):
@@ -348,40 +348,66 @@
         t0_copy(k).start()
         d_send(k)
 
-    for j in range(NJ):
-        z_copy(j).start()
+    def own_start(j):
         for d in range(2):
             x_copy(j, 0, d).start()
+
+    def z_next(j):
+        z_copy(j - 1).wait_send()
+        z_copy(j).start()
+
+    z_copy(0).start()
+    own_start(0)
+    own_start(1)
     prepare()
+    z_next(1)
+    x_forward(0, 0)
+    own_start(2)
     choose()
     diag_load.wait()
-    x_forward(0, 0)
     z_forward(0)
+    z_next(2)
     x_forward(1, 0)
-    for j in range(NJ):
-        x_forward(j, 1)
-        if j + 1 < NJ:
-            z_forward(j + 1)
-        if j + 2 < NJ:
-            x_forward(j + 2, 0)
-        f_wait(j)
-        multiply(j)
-        if j >= 1:
-            l_mid(j - 1)
-        c_sum(j)
-        if j >= 1:
-            l_end(j - 1)
-            output(j - 1)
-        if j == 2:
-            sum_start(0)
-        if j == 3:
-            t1_send(0)
-    l_mid(NJ - 1)
+    x_forward(0, 1)
+    own_start(3)
+    z_forward(1)
+    z_next(3)
+    x_forward(2, 0)
+    f_wait(0)
+    multiply(0)
+    x_forward(1, 1)
+    c_sum(0)
+    z_forward(2)
+    x_forward(3, 0)
+    f_wait(1)
+    multiply(1)
+    x_forward(2, 1)
+    z_forward(3)
+    l_mid(0)
+    c_sum(1)
+    f_wait(2)
+    multiply(2)
+    x_forward(3, 1)
+    l_end(0)
+    output(0)
+    l_mid(1)
+    c_sum(2)
+    f_wait(3)
+    multiply(3)
+    l_end(1)
+    output(1)
+    sum_start(0)
+    c_sum(3)
+    l_mid(2)
+    t1_send(0)
+    l_end(2)
+    output(2)
     t2_send(0)
-    l_end(NJ - 1)
-    output(NJ - 1)
+    l_mid(3)
+    t3_send(0)
+    l_end(3)
+    output(3)
     sum_start(1)
-    t3_send(0)
     t1_send(1)
     t4_send(0)
     t2_send(1)
@@ -396,7 +422,8 @@
         for copy in (t0_copy(k), t1_all(k), t2_all(k), t3_all(k), t4_copy(k), d_all(k)):
             copy.wait_send()
     for j in range(NJ):
-        z_copy(j).wait_send()
+        if j == NJ - 1:
+            z_copy(j).wait_send()
         for h in range(2):
             for d in range(2):
                 x_copy(j, h, d).wait_send()
@@ -438,7 +465,7 @@
             pltpu.VMEM((2, 16, 8, 256), F32),
             pltpu.VMEM((2, 15, 8, 256), F32),
             pltpu.VMEM((2, 8, 8, 256), F32),
-            pltpu.VMEM((64, 128), F32),
+            pltpu.VMEM((128, 64), F32),
             pltpu.VMEM((2, 4, 32, 256), F32),
             pltpu.VMEM((2, 3, 32, 256), F32),
             pltpu.VMEM((2, 2, 512, 512), BF16),
@@ -464,10 +491,34 @@
     )(tiles, diag, factor, pattern, owner, anc, order, table)
 
 
+def finish_kernel(rows, dens, zed, rows_out, dens_out, zed_out):
+    rows_out[...] = rows[...]
+    dens_out[...] = dens[...]
+    zed_out[...] = zed[...]
+
+
+def finish_call(rows, dens, zed):
+    vmem = pl.BlockSpec(memory_space=pltpu.VMEM)
+    return pl.pallas_call(
+        finish_kernel,
+        out_shape=tuple(jax.ShapeDtypeStruct(v.shape, v.dtype) for v in (rows, dens, zed)),
+        in_specs=[vmem] * 3,
+        out_specs=(vmem,) * 3,
+    )(rows, dens, zed)
+
+
 def shards(tiles, factor, diag, pattern, anc, row_owner, table, order):
     rows, dens, zed = main_call(
-        tiles, diag.reshape(2, 2, 2, 32, 8, 256), factor, pattern, row_owner, anc, order, table
+        tiles,
+        diag.reshape(2, 2, 2, 32, 8, 256),
+        factor,
+        pattern,
+        row_owner.reshape(1, 64),
+        anc,
+        order,
+        table.T,
     )
+    rows, dens, zed = finish_call(rows, dens, zed)
     return rows, dens[None], zed.reshape(2, 256, 256)
 
 

time: 124 us -> 102 us (0.82)
  Pallas kernels: 115 us -> 101 us
  local copies, waits for them, and re-layouts: 7.91 us -> 0 us
    pallas_call x1, Pallas kernels: 115 us -> 98.7 us  [main_call(): pl.pallas_call(main_kernel, out_shape=(jax.ShapeDtypeStruct((2, 2, 64, 51...]
    unnamed x5 -> x0, local copies, waits for them, and re-layouts: 7.91 us -> none
    pallas_call x0 -> x1, Pallas kernels: none -> 2.24 us  [finish_call(): pl.pallas_call(finish_kernel, out_shape=tuple((jax.ShapeDtypeStruct(v.sha...]
where the time goes in v2:
time: 102 us
  Pallas kernels  101 us (99%)
    pallas_call x1, Pallas kernels, main_call(): pl.pallas_call(main_kernel, out_shape=(jax.ShapeDtypeStruct((2, 2, 64, 51...  98.7 us
    pallas_call x1, Pallas kernels, finish_call(): pl.pallas_call(finish_kernel, out_shape=tuple((jax.ShapeDtypeStruct(v.sha...  2.24 us

profile of v2, /device:TPU:1, one launch (start us, length us, event | category | flops | bytes accessed | tf_op | source)
XLA Modules:
  0.0 101.6 jit_solution(15159854109938029275)
XLA Ops:
  0.6 98.7 %shard_map.103 = (f32[2,2,64,512]{3,2,1,0:T(8,128)}, f32[32,512]{1,0:T(8,128)}, f32[2,32,8,256]{3,2,1,0:T(8,128)}) custom-call(f32[2,2,8,64,512]{4,3,2,1,0:T(8,128)} %tiles_hbm.1, f32[2,2,2,32,8,256]{5,4,3,2,1,0:T(8,128)} %bitcast.5, f32[2,2,64,512]{3,2,1,0:T(8,128)} %factor.1, s32[64,64]{1,0:T(8,128)} %pattern.1, s32[1,64]{1,0:T(1,128)} %bitcast.7, ...), custom_call_target="tpu_custom_call" | custom-call | tf_op jit(solution)/shard_map/pallas_call | solution.py:450
  99.3 2.2 %shard_map.104 = (f32[2,2,64,512]{3,2,1,0:T(8,128)}, f32[32,512]{1,0:T(8,128)}, f32[2,32,8,256]{3,2,1,0:T(8,128)}) custom-call(f32[2,2,64,512]{3,2,1,0:T(8,128)} %get-tuple-element.9.rows, f32[32,512]{1,0:T(8,128)} %get-tuple-element.10.dens, f32[2,32,8,256]{3,2,1,0:T(8,128)} %get-tuple-element.11.zed), custom_call_target="tpu_custom_call" | custom-call | tf_op jit(solution)/shard_map/pallas_call | solution.py:502

commit v3 on v2

--- a/solution.py
+++ b/solution.py
@@ -8,8 +8,9 @@
 from jax.sharding import PartitionSpec as P
 
 MESH = pl.DeviceIdType.MESH
-JOBS = ((0, 0), (1, 0), (0, 1), (1, 1))
+JOBS = ((0, 0, 0, 2), (1, 0, 0, 2), (0, 1, 0, 2), (1, 1, 0, 2))
 NJ = len(JOBS)
+EARLY = 1
 F32, BF16 = jnp.float32, jnp.bfloat16
 
 
@@ -25,9 +26,9 @@
 def main_kernel(
     tiles_hbm, diag_hbm, factor, pattern, owner, anc, order, table,
     rows_out, dens_out, zed_out,
-    tiles, diag, dens, zed, zcross, zpart, zplane, zline, chosen, picked, dgot, a_high, a_low, gath, l_high, l_low, prod, cross, sums, line, tile_sem, diag_sem,
+    tiles, diag, dens, zed, zcross, zpart, zplane, zline, chosen, picked, dgot, peers_l, a_high, a_low, gath, l_high, l_low, prod, cross, sums, line, tile_sem, diag_sem,
     zs, zr, xs, xr, fs, fr, cs, cr, ls, lr,
-    t0s, t0r, t1s, t1r, t2s, t2r, t3s, t3r, t4s, t4r, ds, dr,
+    gs, gr, t0s, t0r, t1s, t1r, t2s, t2r, t3s, t3r, t4s, t4r, ds, dr,
 ):
     pole, row, col = lax.axis_index("pole"), lax.axis_index("row"), lax.axis_index("col")
     zl, core = row // 2, row % 2
@@ -78,8 +79,12 @@
 
     block = row * 8 + col
     keeps = [anc[k, block].astype(F32) for k in range(2)]
-    for j, (p, k) in enumerate(JOBS):
-        gath[j, col] = factor[p, :, :, k * 256 : (k + 1) * 256] * keeps[k]
+    zed[...] = jnp.zeros_like(zed)
+    for p in range(2):
+        for k in range(2):
+            for h in range(2):
+                first = k * 256 + h * 128
+                gath[k * 2 + p, col, h] = factor[p, :, :, first : first + 128] * keeps[k]
 
     pl.semaphore_wait(barrier, 23)
 
@@ -88,16 +93,24 @@
             src_ref=src, dst_ref=dst, send_sem=send, recv_sem=recv, device_id=peer, device_id_type=MESH
         )
 
+    def view(ref, j, *at):
+        p, k, first, count = JOBS[j]
+        return ref.at[(k * 2 + p, *at, pl.ds(first, count))]
+
+    def half_view(j, slot, d):
+        p, k, first, count = JOBS[j]
+        return gath.at[k * 2 + p, slot, d] if count == 2 else gath.at[k * 2 + p, slot, first, d]
+
     def z_copy(j):
-        return remote(gath.at[j, col], gath.at[j, col], zs.at[j], zr.at[j], partner)
+        return remote(view(gath, j, col), view(gath, j, col), zs.at[j], zr.at[j], partner)
 
     def z_recv(j):
-        return remote(gath.at[j, other_col], gath.at[j, other_col], zs.at[j], zr.at[j], partner)
+        return remote(view(gath, j, other_col), view(gath, j, other_col), zs.at[j], zr.at[j], partner)
 
     def x_copy(j, h, d):
         slot = col if h == 0 else other_col
         peer = right if d == 0 else left
-        return remote(gath.at[j, slot], gath.at[j, slot], xs.at[j, h, d], xr.at[j, h, d], peer)
+        return remote(view(gath, j, slot), view(gath, j, slot), xs.at[j, h, d], xr.at[j, h, d], peer)
 
     def x_slot(h, shift):
         half_of = zh if h == 0 else 1 - zh
@@ -105,16 +118,16 @@
 
     def x_recv(j, h, d):
         slot = x_slot(h, 3 if d == 0 else 1)
-        return remote(gath.at[j, slot], gath.at[j, slot], xs.at[j, h, d], xr.at[j, h, d], right)
+        return remote(view(gath, j, slot), view(gath, j, slot), xs.at[j, h, d], xr.at[j, h, d], right)
 
     def f_copy(j, h, d):
         slot = x_slot(h, 3 if d == 0 else 1)
         peer = right if d == 0 else left
-        return remote(gath.at[j, slot, d], gath.at[j, slot, d], fs.at[j, h, d], fr.at[j, h, d], peer)
+        return remote(half_view(j, slot, d), half_view(j, slot, d), fs.at[j, h, d], fr.at[j, h, d], peer)
 
     def f_recv(j, h, d):
         slot = x_slot(h, 2)
-        return remote(gath.at[j, slot, d], gath.at[j, slot, d], fs.at[j, h, d], fr.at[j, h, d], right)
+        return remote(half_view(j, slot, d), half_view(j, slot, d), fs.at[j, h, d], fr.at[j, h, d], right)
 
     def z_forward(j):
         z_recv(j).wait_recv()
@@ -154,54 +167,64 @@
             lax.fori_loop(0, 4, one, 0)
 
     def multiply(j):
-        p, k = JOBS[j]
+        p, k, first, count = JOBS[j]
+        b = k * 2 + p
 
         def halves(c, carry):
-            for part in range(2):
-                high, low = split(gath[j, c, part])
-                at = pl.ds(pl.multiple_of(c * 64, 64), 64)
-                l_high[part, at] = high
-                l_low[part, at] = low
-                if part == 1:
-                    l_high[2, at] = -high
-                    l_low[2, at] = -low
+            at = pl.ds(pl.multiple_of(c * 64, 64), 64)
+            for h in range(first, first + count):
+                for part in range(2):
+                    high, low = split(gath[b, c, h, part])
+                    same = slice(h * 256 + part * 128, h * 256 + part * 128 + 128)
+                    turned = slice(h * 256 + 128 - part * 128, h * 256 + 256 - part * 128)
+                    l_high[0, at, same] = high
+                    l_low[0, at, same] = low
+                    l_high[1, at, turned] = -high if part else high
+                    l_low[1, at, turned] = -low if part else low
             return carry
 
         lax.fori_loop(0, 8, halves, 0)
 
-        def one(n, carry):
+        def one(h, carry):
+            at = pl.ds(pl.multiple_of(h * 256, 256), 256)
             total = None
             for part in range(2):
-                pick = part * 2 * (1 - n) + (1 - part) * n
-                bh, bl = l_high[pick], l_low[pick]
+                bh, bl = l_high[part, :, at], l_low[part, :, at]
                 ah, al = a_high[p, part], a_low[p, part]
                 term = dot(ah, bh) + (dot(ah, bl) + dot(al, bh))
                 total = term if total is None else total + term
             for g in range(8):
-                prod[j, g, n] = total[g * 64 : (g + 1) * 64]
+                rows = total[g * 64 : (g + 1) * 64]
+                prod[b, g, h, 0] = rows[:, :128]
+                prod[b, g, h, 1] = rows[:, 128:]
             return carry
 
-        lax.fori_loop(0, 2, one, 0)
+        lax.fori_loop(first, first + count, one, 0)
         for d in range(4):
             c_copy(j, d).start()
 
     def c_copy(j, d):
-        return remote(prod.at[j, d * 2 + 1 - core], cross.at[j, d], cs.at[j, d], cr.at[j, d], sibling)
+        return remote(
+            view(prod, j, d * 2 + 1 - core), view(cross, j, d), cs.at[j, d], cr.at[j, d], sibling
+        )
 
     def at_line(d):
         return d + half * (3 - 2 * d)
 
     def l_copy(j, slot, d, peer):
-        return remote(sums.at[j, d], line.at[j, slot], ls.at[j, d], lr.at[j, slot], peer)
+        return remote(view(sums, j, d), view(line, j, slot), ls.at[j, d], lr.at[j, slot], peer)
 
     def l_wait(j, slot):
-        remote(sums.at[j, 0], line.at[j, slot], ls.at[j, 0], lr.at[j, slot], mate).wait_recv()
+        l_copy(j, slot, 0, mate).wait_recv()
+        return view(line, j, slot)[...]
 
     def c_sum(j):
         for d in (3, 2, 1, 0):
             place = at_line(d)
-            remote(prod.at[j, 0], cross.at[j, place], cs.at[j, d], cr.at[j, place], sibling).wait_recv()
-            sums[j, d] = prod[j, place * 2 + core] + cross[j, place]
+            remote(
+                view(prod, j, 0), view(cross, j, place), cs.at[j, d], cr.at[j, place], sibling
+            ).wait_recv()
+            view(sums, j, d)[...] = view(prod, j, place * 2 + core)[...] + view(cross, j, place)[...]
             if d > 0:
 
                 @pl.when(inner == 0)
@@ -212,46 +235,113 @@
         @pl.when(inner == 1)
         def _():
             for d in (3, 2):
-                l_wait(j, d - 1)
-                sums[j, d] = sums[j, d] + line[j, d - 1]
+                here = view(sums, j, d)
+                here[...] = here[...] + l_wait(j, d - 1)
                 l_copy(j, 6 - d, d, across).start()
 
     def l_end(j):
         @pl.when(inner == 1)
         def _():
-            l_wait(j, 3)
-            sums[j, 0] = sums[j, 0] + line[j, 3]
+            here = view(sums, j, 0)
+            here[...] = here[...] + l_wait(j, 3)
             l_copy(j, 3, 0, mate).start()
-            l_wait(j, 0)
-            l_wait(j, 4)
-            sums[j, 1] = sums[j, 1] + (line[j, 0] + line[j, 4])
+            here = view(sums, j, 1)
+            here[...] = here[...] + (l_wait(j, 0) + l_wait(j, 4))
 
         @pl.when(inner == 0)
         def _():
-            l_wait(j, 3)
-            sums[j, 0] = sums[j, 0] + line[j, 3]
+            here = view(sums, j, 0)
+            here[...] = here[...] + l_wait(j, 3)
 
     def output(j):
-        p, k = JOBS[j]
-        at = slice(k * 256, (k + 1) * 256)
-        done = sums[j, inner] * keeps[k]
-        rows_out[p, :, :, at] = done
+        p, k, first, count = JOBS[j]
         entry = order[pole * 2 + p]
         wr, wi = table[0, entry], table[1, entry]
-        fr_, fi_ = gath[j, col, 0], gath[j, col, 1]
-        density = wr * done[1] + wi * done[0]
-        left_side = jnp.concatenate([wr * fi_ + wi * fr_, wr * fr_ - wi * fi_], axis=0)
-        right_side = jnp.concatenate([done[0], done[1]], axis=0)
-        product = lax.dot_general(
-            left_side, right_side, (((0,), (0,)), ((), ())),
-            precision=lax.Precision.HIGHEST, preferred_element_type=F32,
-        ).reshape(32, 8, 256)
-        if p == 0:
-            dens[k] = density
-            zed[k] = -product
-        else:
-            dens[k] += density
-            zed[k] -= product
+        done = view(sums, j, inner)[...] * keeps[k]
+        for i in range(count):
+            lanes = slice((first + i) * 128, (first + i + 1) * 128)
+            rows_out[p, :, :, k * 256 + lanes.start : k * 256 + lanes.stop] = done[i]
+            density = wr * done[i, 1] + wi * done[i, 0]
+            if p == 0:
+                dens[k, :, lanes] = density
+            else:
+                dens[k, :, lanes] += density
+        if k != EARLY:
+            zed_add(j, weighted(gath[k * 2 + p, col], p), done)
+
+    def weighted(block, p):
+        entry = order[pole * 2 + p]
+        wr, wi = table[0, entry], table[1, entry]
+        panels = [
+            jnp.concatenate(
+                [wr * block[h, 1] + wi * block[h, 0], wr * block[h, 0] - wi * block[h, 1]], axis=0
+            )
+            for h in range(2)
+        ]
+        return jnp.concatenate(panels, axis=1)
+
+    def zed_add(j, left_side, values):
+        p, k, first, count = JOBS[j]
+        for i in range(count):
+            product = lax.dot_general(
+                left_side, values[i].reshape(128, 128), (((0,), (0,)), ((), ())),
+                precision=lax.Precision.HIGHEST, preferred_element_type=F32,
+            ).reshape(32, 8, 128)
+            zed[k, :, :, (first + i) * 128 : (first + i + 1) * 128] -= product
+
+    def g_copy(p, source, place, at, peer):
+        return remote(source, peers_l.at[p, place], gs.at[p, at], gr.at[p, place], peer)
+
+    def g_own(p, at, peer):
+        return g_copy(p, gath.at[2 + p, col], zl, at, peer)
+
+    def g_wait(p, d):
+        g_copy(p, gath.at[2 + p, col], at_line(d), 0, mate).wait_recv()
+
+    def g_pass(p, d, at, peer):
+        place = at_line(d)
+        return g_copy(p, peers_l.at[p, place], place, at, peer)
+
+    def g_start(p):
+        peers_l[p, zl] = gath[2 + p, col]
+
+        @pl.when(inner == 0)
+        def _():
+            g_own(p, 0, mate).start()
+
+        @pl.when(inner == 1)
+        def _():
+            g_own(p, 0, across).start()
+            g_own(p, 1, mate).start()
+
+    def g_mid(p):
+        @pl.when(inner == 1)
+        def _():
+            g_wait(p, 0)
+            g_pass(p, 0, 2, across).start()
+            g_wait(p, 2)
+            g_pass(p, 2, 3, mate).start()
+
+    def g_far(p):
+        @pl.when(inner == 1)
+        def _():
+            g_wait(p, 3)
+            g_pass(p, 3, 4, mate).start()
+
+    def g_end(p):
+        @pl.when(inner == 0)
+        def _():
+            for d in (1, 2, 3):
+                g_wait(p, d)
+
+    def zed_early(j):
+        p = JOBS[j][0]
+
+        def one(d, carry):
+            zed_add(j, weighted(peers_l[p, at_line(d)], p), view(sums, j, d)[...])
+            return carry
+
+        lax.fori_loop(0, 4, one, 0)
 
     def choose():
         lines = lax.broadcasted_iota(jnp.int32, (128, 64), 0)
@@ -343,10 +433,6 @@
     def t4_send(k):
         t3_all(k).wait_recv()
         t4_copy(k).start()
-
-    def sum_start(k):
-        t0_copy(k).start()
-        d_send(k)
 
     def own_start(j):
         for d in range(2):
@@ -366,12 +452,13 @@
     choose()
     diag_load.wait()
     z_forward(0)
-    z_next(2)
+    z_copy(2).start()
     x_forward(1, 0)
     x_forward(0, 1)
     own_start(3)
     z_forward(1)
-    z_next(3)
+    z_copy(3).start()
+    g_start(0)
     x_forward(2, 0)
     f_wait(0)
     multiply(0)
@@ -379,10 +466,12 @@
     c_sum(0)
     z_forward(2)
     x_forward(3, 0)
+    g_start(1)
     f_wait(1)
     multiply(1)
     x_forward(2, 1)
     z_forward(3)
+    g_mid(0)
     l_mid(0)
     c_sum(1)
     f_wait(2)
@@ -390,39 +479,58 @@
     x_forward(3, 1)
     l_end(0)
     output(0)
+    g_mid(1)
     l_mid(1)
     c_sum(2)
+    g_far(0)
+    g_end(0)
+    zed_early(2)
     f_wait(3)
     multiply(3)
+    g_far(1)
     l_end(1)
     output(1)
-    sum_start(0)
+    t0_copy(0).start()
+    d_send(0)
     c_sum(3)
+    g_end(1)
+    zed_early(3)
+    t0_copy(1).start()
+    t1_send(0)
     l_mid(2)
-    t1_send(0)
+    t1_send(1)
     l_end(2)
     output(2)
     t2_send(0)
+    t2_send(1)
     l_mid(3)
     t3_send(0)
+    t3_send(1)
     l_end(3)
     output(3)
-    sum_start(1)
-    t1_send(1)
+    d_send(1)
     t4_send(0)
-    t2_send(1)
+    t4_send(1)
     d_take(0)
-    d_take(1)
-    t3_send(1)
-    t4_send(1)
     for k in range(2):
         t4_copy(k).wait_recv()
+    d_take(1)
 
     for k in range(2):
         for copy in (t0_copy(k), t1_all(k), t2_all(k), t3_all(k), t4_copy(k), d_all(k)):
             copy.wait_send()
+    for p in range(2):
+        g_own(p, 0, mate).wait_send()
+
+        @pl.when(inner == 1)
+        def _(p=p):
+            for at in range(1, 5):
+                g_own(p, at, mate).wait_send()
+
+
+    z_copy(NJ - 1).wait_send()
     for j in range(NJ):
-        if j == NJ - 1:
+        if j in (1, 2):
             z_copy(j).wait_send()
         for h in range(2):
             for d in range(2):
@@ -468,21 +576,23 @@
             pltpu.VMEM((128, 64), F32),
             pltpu.VMEM((2, 4, 32, 256), F32),
             pltpu.VMEM((2, 3, 32, 256), F32),
+            pltpu.VMEM((2, 4, 2, 2, 64, 128), F32),
             pltpu.VMEM((2, 2, 512, 512), BF16),
             pltpu.VMEM((2, 2, 512, 512), BF16),
-            pltpu.VMEM((NJ, 8, 2, 64, 256), F32),
-            pltpu.VMEM((3, 512, 256), BF16),
-            pltpu.VMEM((3, 512, 256), BF16),
-            pltpu.VMEM((NJ, 8, 2, 64, 256), F32),
-            pltpu.VMEM((NJ, 4, 2, 64, 256), F32),
-            pltpu.VMEM((NJ, 4, 2, 64, 256), F32),
-            pltpu.VMEM((NJ, 5, 2, 64, 256), F32),
+            pltpu.VMEM((4, 8, 2, 2, 64, 128), F32),
+            pltpu.VMEM((2, 512, 512), BF16),
+            pltpu.VMEM((2, 512, 512), BF16),
+            pltpu.VMEM((4, 8, 2, 2, 64, 128), F32),
+            pltpu.VMEM((4, 4, 2, 2, 64, 128), F32),
+            pltpu.VMEM((4, 4, 2, 2, 64, 128), F32),
+            pltpu.VMEM((4, 5, 2, 2, 64, 128), F32),
             dma, dma,
             dma((NJ,)), dma((NJ,)),
             dma((NJ, 2, 2)), dma((NJ, 2, 2)),
             dma((NJ, 2, 2)), dma((NJ, 2, 2)),
             dma((NJ, 4)), dma((NJ, 4)),
             dma((NJ, 4)), dma((NJ, 5)),
+            dma((2, 5)), dma((2, 4)),
             *([dma((2,))] * 12),
         ],
         compiler_params=pltpu.CompilerParams(

time: 102 us -> 94.4 us (0.925)
  Pallas kernels: 101 us -> 93.7 us
    pallas_call x1, Pallas kernels: 98.7 us -> 91.4 us  [main_call(): pl.pallas_call(main_kernel, out_shape=(jax.ShapeDtypeStruct((2, 2, 64, 51...]
where the time goes in v3:
time: 94.4 us; the launch traced here: 94.3 us
  Pallas kernels  93.7 us (99%)
    pallas_call x1, Pallas kernels, main_call(): pl.pallas_call(main_kernel, out_shape=(jax.ShapeDtypeStruct((2, 2, 64, 51...  91.4 us
    pallas_call x1, Pallas kernels, finish_call(): pl.pallas_call(finish_kernel, out_shape=tuple((jax.ShapeDtypeStruct(v.sha...  2.24 us

profile of v3, /device:TPU:1, one launch (start us, length us, event | category | flops | bytes accessed | tf_op | source)
XLA Modules:
  0.0 94.3 jit_solution(3495243824188917148)
XLA Ops:
  0.6 91.4 %shard_map.103 = (f32[2,2,64,512]{3,2,1,0:T(8,128)}, f32[32,512]{1,0:T(8,128)}, f32[2,32,8,256]{3,2,1,0:T(8,128)}) custom-call(f32[2,2,8,64,512]{4,3,2,1,0:T(8,128)} %tiles_hbm.1, f32[2,2,2,32,8,256]{5,4,3,2,1,0:T(8,128)} %bitcast.5, f32[2,2,64,512]{3,2,1,0:T(8,128)} %factor.1, s32[64,64]{1,0:T(8,128)} %pattern.1, s32[1,64]{1,0:T(1,128)} %bitcast.7, ...), custom_call_target="tpu_custom_call" | custom-call | tf_op jit(solution)/shard_map/pallas_call | solution.py:558
  92.1 2.2 %shard_map.104 = (f32[2,2,64,512]{3,2,1,0:T(8,128)}, f32[32,512]{1,0:T(8,128)}, f32[2,32,8,256]{3,2,1,0:T(8,128)}) custom-call(f32[2,2,64,512]{3,2,1,0:T(8,128)} %get-tuple-element.9.rows, f32[32,512]{1,0:T(8,128)} %get-tuple-element.10.dens, f32[2,32,8,256]{3,2,1,0:T(8,128)} %get-tuple-element.11.zed), custom_call_target="tpu_custom_call" | custom-call | tf_op jit(solution)/shard_map/pallas_call | solution.py:612

commit v4 on v3

--- a/solution.py
+++ b/solution.py
@@ -492,12 +492,12 @@
     output(1)
     t0_copy(0).start()
     d_send(0)
+    l_mid(2)
     c_sum(3)
     g_end(1)
     zed_early(3)
     t0_copy(1).start()
     t1_send(0)
-    l_mid(2)
     t1_send(1)
     l_end(2)
     output(2)

time: 94.4 us -> 94.4 us (level)
  no operation moved by 1% of the time
where the time goes in v4:
time: 94.4 us; the launch traced here: 94.3 us
  Pallas kernels  93.7 us (99%)
    pallas_call x1, Pallas kernels, main_call(): pl.pallas_call(main_kernel, out_shape=(jax.ShapeDtypeStruct((2, 2, 64, 51...  91.4 us
    pallas_call x1, Pallas kernels, finish_call(): pl.pallas_call(finish_kernel, out_shape=tuple((jax.ShapeDtypeStruct(v.sha...  2.24 us

profile of v4, /device:TPU:1, one launch (start us, length us, event | category | flops | bytes accessed | tf_op | source)
XLA Modules:
  0.0 94.3 jit_solution(7576452832388058873)
XLA Ops:
  0.6 91.4 %shard_map.103 = (f32[2,2,64,512]{3,2,1,0:T(8,128)}, f32[32,512]{1,0:T(8,128)}, f32[2,32,8,256]{3,2,1,0:T(8,128)}) custom-call(f32[2,2,8,64,512]{4,3,2,1,0:T(8,128)} %tiles_hbm.1, f32[2,2,2,32,8,256]{5,4,3,2,1,0:T(8,128)} %bitcast.5, f32[2,2,64,512]{3,2,1,0:T(8,128)} %factor.1, s32[64,64]{1,0:T(8,128)} %pattern.1, s32[1,64]{1,0:T(1,128)} %bitcast.7, ...), custom_call_target="tpu_custom_call" | custom-call | tf_op jit(solution)/shard_map/pallas_call | solution.py:558
  92.1 2.2 %shard_map.104 = (f32[2,2,64,512]{3,2,1,0:T(8,128)}, f32[32,512]{1,0:T(8,128)}, f32[2,32,8,256]{3,2,1,0:T(8,128)}) custom-call(f32[2,2,64,512]{3,2,1,0:T(8,128)} %get-tuple-element.9.rows, f32[32,512]{1,0:T(8,128)} %get-tuple-element.10.dens, f32[2,32,8,256]{3,2,1,0:T(8,128)} %get-tuple-element.11.zed), custom_call_target="tpu_custom_call" | custom-call | tf_op jit(solution)/shard_map/pallas_call | solution.py:612
